TPU v7x, 768 devices: a whole 4x8x12 slice. The times are simulated.
768 devices in a mesh: section: 3 (over z_lo), dp: 16 (over z_hi, x), expert: 16 (over y, core).
Axes of the slice: x: 4, y: 8, z: 12 (z_hi: 4, z_lo: 3; z = z_hi * 3 + z_lo), core: 2. Of those that a mesh axis runs over, the one named last changes fastest.
Arguments:
- grad_out: bfloat16 [3, 32768, 2048], P('section', ('dp', 'expert')), may hold values from -6 to 6
- routes: int32 [3, 32768, 2], P('section', ('dp', 'expert')), may hold values from 0 to 15, all different within a row; in each aligned block of 128 rows (0 to 127, 128 to 255, ..., all dimensions but the last counted through in order) at most 20 rows name the same one
- gates: float32 [3, 32768, 2], P('section', ('dp', 'expert')), may hold values from 0.2 to 1
- hidden: bfloat16 [3, 16, 16, 320, 1408], P('section', 'dp', 'expert'), may hold values from -0.09375 to 0.09375
- w_down: bfloat16 [3, 16, 1408, 2048], P('section', 'expert'), may hold values from -0.15625 to 0.15625
Outputs:
- grad_hidden: bfloat16 [3, 16, 16, 320, 1408], P('section', 'dp', 'expert')
- grad_w_down: float32 [3, 16, 1408, 2048], P('section', 'expert', 'dp')
Inputs may be any that keep to these rules, and one draw needn't show every extreme that they name: `routes`: each token names 2 different experts; among the 128 tokens of one device no expert is named more than 20 times, a bound that some block reaches.
All inputs are finite; a program needn't handle non-finite values.
Results may differ from a plain program's by a relative error of at most 0.015.
Values may be sent and summed in bfloat16 or wider, within the bound.
A program may use at most 64 MiB of HBM per device.

v0:
```python
import jax
import jax.numpy as jnp
from jax import lax
from jax.sharding import PartitionSpec as P


def shifted(value, axis, steps):
    count = lax.axis_size(axis)
    pairs = [(source, (source + steps) % count) for source in range(count)]
    return lax.ppermute(value, axis, pairs)


def dispatch_block(rows, ids, weights, count, width):
    flat_ids = ids.reshape(-1)
    onehot = (flat_ids[:, None] == jnp.arange(count, dtype=jnp.int32)[None, :]).astype(jnp.int32)
    position = jnp.sum((jnp.cumsum(onehot, axis=0) - 1) * onehot, axis=1)
    target = flat_ids * width + position
    scaled = (weights[:, :, None] * rows[:, None, :].astype(jnp.float32)).astype(jnp.bfloat16)
    scaled = scaled.reshape(-1, rows.shape[1])
    buffer = jnp.zeros((count * width, rows.shape[1]), jnp.bfloat16).at[target].set(scaled)
    return buffer.reshape(count, width, rows.shape[1])


def shards(grad_out, routes, gates, hidden, w_down):
    incoming = shifted(grad_out, "section", -1)[0]
    groups = lax.axis_size("expert")
    saved = hidden[0, 0, 0]
    weight = w_down[0, 0]
    slot_count = saved.shape[0]
    width = slot_count // groups
    model_width = incoming.shape[1]
    outgoing = dispatch_block(incoming, routes[0], gates[0], groups, width)
    piece = lax.all_to_all(outgoing, "expert", split_axis=0, concat_axis=0, tiled=True)
    grad_rows_out = jnp.einsum(
        "skd,hd->skh", piece, weight, preferred_element_type=jnp.float32
    ).astype(jnp.bfloat16)
    scaled = piece.reshape(slot_count, model_width)
    full = lax.dot_general(
        saved, scaled, (((0,), (0,)), ((), ())), preferred_element_type=jnp.float32
    )
    weight_grad = lax.psum_scatter(
        full.astype(jnp.bfloat16), "dp", scatter_dimension=0, tiled=True
    ).astype(jnp.float32)
    grad_hidden = grad_rows_out.reshape(1, 1, 1, slot_count, saved.shape[1])
    return (grad_hidden, weight_grad.reshape(1, 1, weight_grad.shape[0], model_width))


def solution(mesh):
    placed = (
        P("section", ("dp", "expert"), None),
        P("section", ("dp", "expert"), None),
        P("section", ("dp", "expert"), None),
        P("section", "dp", "expert", None, None),
        P("section", "expert", None, None),
    )
    return jax.shard_map(
        shards,
        mesh=mesh,
        in_specs=placed,
        out_specs=(P("section", "dp", "expert", None, None), P("section", "expert", "dp", None)),
        check_vma=False,
    )
```

profile of v0, /device:TPU:1, one launch (start us, length us, event | category | flops | bytes accessed | tf_op | source)
XLA Modules:
  0.0 258.2 jit_solution(8037807867886126269)
XLA Ops:
  7.2 0.0 copy-start
  7.2 0.0 reduce-scatter.4.cloned.1.call-start
  7.2 6.8 %collective-permute-start = (bf16[1,128,2048]{2,1,0:T(8,128)(2,1)}, bf16[1,128,2048]{2,1,0:T(8,128)(2,1)S(1)}, u32[]{:S(2)}, u32[]{:S(2)}) collective-permute-start(bf16[1,128,2048]{2,1,0:T(8,128)(2,1)} %param.5), channel_id=1, source_target_pairs={{0,512},{256,0},{512,256},{1,513},{257,1},{513,257},{2,514},{258,2... | collective-permute-start | bytes 1572872 | tf_op jit(solution)/shard_map/ppermute | solution.py:10
  14.0 0.8 copy.15
  14.8 0.1 eq.29
  14.9 0.7 broadcast_multiply_fusion
  15.6 0.1 eq.25
  15.8 0.1 copy.14
  15.9 0.1 mul.39
  16.0 0.6 reduce-window.6
  16.6 0.2 slice_reduce_fusion
  16.8 0.8 copy.18
  17.6 0.1 mul.41
  17.8 0.1 fusion.11
  17.9 2.6 collective-permute-done
  20.4 0.1 bitcast_convert_fusion.1
  20.5 2.5 mul.43
  23.1 2.7 %mul.44 = f32[256,2048]{1,0:T(8,128)S(1)} reshape(f32[128,2,2048]{2,1,0:T(2,128)} %mul.43) | data formatting | bytes 4194304 | tf_op jit(solution)/shard_map/mul | solution.py:18
  25.8 3.4 %scatter_custom_fusion = bf16[320,2048]{1,0:T(8,128)(2,1)} fusion(s32[256]{0:T(256)S(1)} %bitcast.40, f32[256,2048]{1,0:T(8,128)S(1)} %mul.44, f32[256]{0:T(256)S(1)} %mul.41, bf16[]{:T(256)} %constant.5.clone.1), kind=kCustom, calls=%fused_computation.7 | custom fusion | flops 1048576 | bytes 3408898 | tf_op jit(solution)/shard_map/scatter | solution.py:20
  29.1 3.2 %reshape.81 = bf16[16,20,2048]{2,1,0:T(8,128)(2,1)} reshape(bf16[320,2048]{1,0:T(8,128)(2,1)} %scatter_custom_fusion) | data formatting | bytes 2621440 | tf_op jit(solution)/shard_map/reshape | solution.py:21
  32.3 52.9 %all_to_all.5 = bf16[16,20,2048]{2,1,0:T(8,128)(2,1)S(1)} all-to-all(bf16[16,20,2048]{2,1,0:T(8,128)(2,1)} %reshape.81), channel_id=1, replica_groups=mesh['section'=3,'dp'=16,'expert'=16] {'expert'}, dimensions={0} | all-to-all | bytes 2621440 | tf_op jit(solution)/shard_map/all_to_all | solution.py:33
  85.2 1.2 reshape.83
  86.5 0.0 copy-done
  86.5 7.2 %fusion = bf16[1408,2048]{0,1:T(8,128)(2,1)} fusion(bf16[320,2048]{1,0:T(8,128)(2,1)} %reshape.83, bf16[1,1,1,320,1408]{4,3,2,1,0:T(8,128)(2,1)S(1)} %copy-done), kind=kOutput, calls=%fused_computation.2 | convolution fusion | flops 1848377344 | bytes 7979008 | tf_op jit(solution)/shard_map/dot_general | solution.py:38
  93.6 8.2 %copy.20 = bf16[1408,2048]{1,0:T(8,128)(2,1)} copy(bf16[1408,2048]{0,1:T(8,128)(2,1)} %fusion) | data formatting | bytes 11534336
  101.8 0.0 reduce-scatter.4.cloned.1.call-update
  101.9 5.3 %fusion.3 = bf16[16,20,1408]{2,1,0:T(8,128)(2,1)S(1)} fusion(bf16[16,20,2048]{2,1,0:T(8,128)(2,1)S(1)} %all_to_all.5, bf16[1,1,1408,2048]{3,2,1,0:T(8,128)(2,1)} %param.9), kind=kOutput, calls=%fused_computation.5 | convolution fusion | flops 1845944320 | bytes 7979008 | tf_op jit(solution)/shard_map/skd,hd->skh/dot_general | solution.py:34
  107.1 1.1 reshape.82
  108.2 140.6 %reduce-scatter.4.cloned.1.call-done = bf16[88,2048]{1,0:T(8,128)(2,1)} async-done(((bf16[1408,2048]{1,0:T(8,128)(2,1)}), bf16[88,2048]{1,0:T(8,128)(2,1)}) %reduce-scatter.4.cloned.1.call-update) | async-done | bytes 360464
  248.8 1.3 copy.21
  250.1 0.1 bitcast_convert_fusion
  250.2 1.2 copy.19
  (4 shorter events, 0.1 us)
Async XLA Ops:
  7.2 79.3 %copy-start = (bf16[1,1,1,320,1408]{4,3,2,1,0:T(8,128)(2,1)S(1)}, bf16[1,1,1,320,1408]{4,3,2,1,0:T(8,128)(2,1)}, u32[]{:S(2)}) copy-start(bf16[1,1,1,320,1408]{4,3,2,1,0:T(8,128)(2,1)} %param.8) | copy-start | bytes 2703364
  7.2 241.6 %reduce-scatter.4.cloned.1.call-start = ((), (), s32[]{:S(2)}) async-start(), calls=%async_computation.2 | async-start | bytes 6127616
  7.2 13.2 %collective-permute-start = (bf16[1,128,2048]{2,1,0:T(8,128)(2,1)}, bf16[1,128,2048]{2,1,0:T(8,128)(2,1)S(1)}, u32[]{:S(2)}, u32[]{:S(2)}) collective-permute-start(bf16[1,128,2048]{2,1,0:T(8,128)(2,1)} %param.5), channel_id=1, source_target_pairs={{0,512},{256,0},{512,256},{1,513},{257,1},{513,257},{2,514},{258,2... | collective-permute-start | bytes 1572872 | tf_op jit(solution)/shard_map/ppermute | solution.py:10
Sparse Core Ops, SparseCore 0:
  102.0 146.7 reduce-scatter.3
where the time goes:
time: 259 us; the launch traced here: 258 us
  waiting for transfers between devices  143 us (55%)
  blocking collectives  52.9 us (20%)
  local copies, waits for them, and re-layouts  23.9 us (9%)
  between operations  14.1 us (5%)
  matrix products  12.4 us (5%)
  starting transfers between devices  6.81 us (3%)
  other arithmetic  4.93 us (2%)
    unnamed x2, waiting for transfers between devices  141 us
    all_to_all x1, blocking collectives, shards(): lax.all_to_all(outgoing, 'expert', split_axis=0, concat_axis=0, tiled=True)  52.9 us
    unnamed x7, local copies, waits for them, and re-layouts  12.3 us
    dot_general x1, matrix products, shards(): lax.dot_general(saved, scaled, (((0,), (0,)), ((), ())), preferred_elemen...  7.15 us
    ppermute x1, starting transfers between devices, shifted(): return lax.ppermute(value, axis, pairs)  6.77 us
    mul x3, local copies, waits for them, and re-layouts, dispatch_block(): weights[:, :, None] * rows[:, None, :].astype(jnp.float32)  5.38 us
    dot_general x1, matrix products, shards(): jnp.einsum('skd,hd->skh', piece, weight, preferred_element_type=jnp.float32)  5.26 us
  transfers between devices with their start and end apart: 2, of which 2 were waited for; matrix products, arithmetic and copies ran while one was open for 4% of the time, Pallas kernels for 0%

commit v1 on v0

v1 whole, which is shorter than its diff:
```python
import functools

import jax
import jax.numpy as jnp
from jax import lax
from jax.experimental import pallas as pl
from jax.experimental.pallas import tpu as pltpu
from jax.sharding import PartitionSpec as P

MESH = pl.DeviceIdType.MESH
RING = 4
WIDE = 512
FOLD = 128
TILE = 16
BF16, F32 = jnp.bfloat16, jnp.float32


def iota(shape, dim):
    return lax.broadcasted_iota(jnp.int32, shape, dim)


def ones_where(mask):
    return jnp.where(mask, 1.0, 0.0)


def dot(left, right):
    return jnp.dot(left, right, preferred_element_type=F32)


def kernel(
    counts, grad_ref, routes_ref, gates_ref, hidden_ref, w_ref, gh_ref, dw_ref,
    inc, send, recv, pick_a, pick_b, place_a, place_b, scaled, hid, hid_t, wv, part, xr1, xr2, col, zr1, zr2, ghv, dwv,
    in_sem, shift_s, shift_r, all_s, all_r, x_s, x_r, z_s, z_r, dw_sem, gh_sem,
):
    n_sec, n_dp, n_exp = counts
    tok, width = grad_ref.shape[1:]
    slots, units = hid.shape
    cap = slots // n_exp
    own_rows = units // n_dp
    block = 2 * own_rows
    chunks = width // WIDE
    padded = hid_t.shape[1]
    rows = TILE * n_exp
    half_x = RING // 2 * block
    half_z = (block // TILE + 1) // 2 * TILE

    sec, dp, ex = lax.axis_index("section"), lax.axis_index("dp"), lax.axis_index("expert")
    xi, zi = lax.rem(dp, RING), lax.div(dp, RING)
    x_up, x_down = lax.rem(xi + 1, RING), lax.rem(xi + RING - 1, RING)
    z_up, z_down = lax.rem(zi + 1, RING), lax.rem(zi + RING - 1, RING)
    x_far, z_far = lax.rem(xi + 2, RING), lax.rem(zi + 2, RING)
    to_x_up, to_x_down = {"dp": zi * RING + x_up}, {"dp": zi * RING + x_down}
    to_z_up, to_z_down = {"dp": z_up * RING + xi}, {"dp": z_down * RING + xi}
    before, after = {"section": lax.rem(sec + n_sec - 1, n_sec)}, {"section": lax.rem(sec + 1, n_sec)}

    barrier = pltpu.get_barrier_semaphore()

    def greet(to):
        pl.semaphore_signal(barrier, inc=1, device_id=to, device_id_type=MESH)

    for to in (before, after, to_x_up, to_x_down, to_z_up, to_z_down):
        greet(to)

    def greet_expert(i, carry):
        greet({"expert": lax.rem(ex + i, n_exp)})
        return carry

    lax.fori_loop(1, n_exp, greet_expert, 0)
    load_hidden = pltpu.make_async_copy(hidden_ref.at[0, 0, 0], hid, in_sem.at[0])
    load_w = pltpu.make_async_copy(w_ref.at[0, 0], wv, in_sem.at[1])
    load_hidden.start()
    pl.semaphore_wait(barrier, 6 + n_exp - 1)

    def remote(source, target, send_sem, recv_sem, to):
        return pltpu.make_async_remote_copy(
            src_ref=source, dst_ref=target, send_sem=send_sem, recv_sem=recv_sem, device_id=to, device_id_type=MESH
        )

    shifts = [
        remote(grad_ref.at[0, :, pl.ds(c * WIDE, WIDE)], inc.at[c], shift_s.at[c], shift_r.at[c], before)
        for c in range(chunks)
    ]
    for copy in shifts:
        copy.start()
    load_w.start()

    lane = iota((tok, FOLD), 1)
    named, gates = routes_ref[0].astype(F32), gates_ref[0]
    table = jnp.where(lane == 0, named[:, 0:1], jnp.where(lane == 1, named[:, 1:2], jnp.where(
        lane == 2, gates[:, 0:1], jnp.where(lane == 3, gates[:, 1:2], 0.0))))
    table = table.T
    expert = lax.shift_right_logical(iota((rows, tok), 0), 4).astype(F32)
    place = jnp.bitwise_and(iota((rows, tok), 0), TILE - 1)
    first, second = table[0:1] == expert, table[1:2] == expert
    active = ones_where(first | second)
    gate = jnp.where(first, table[2:3], jnp.where(second, table[3:4], 0.0))
    earlier = ones_where(iota((tok, tok), 0) < iota((tok, tok), 1)).astype(BF16)
    slot = dot(active.astype(BF16), earlier)
    hit_a = jnp.where(slot == place.astype(F32), active, 0.0)
    hit_b = jnp.where(slot == (TILE + jnp.bitwise_and(place, 3)).astype(F32), active, 0.0)
    gate_a = jnp.sum(hit_a * gate, axis=1, keepdims=True)
    gate_b = jnp.sum(hit_b * gate, axis=1, keepdims=True)
    pick_a[...] = hit_a.astype(BF16)
    quarter = lax.shift_right_logical(place, 2)
    for q in range(4):
        pick_b[:, q * tok:(q + 1) * tok] = jnp.where(quarter == q, hit_b, 0.0).astype(BF16)

    def exchange(c, start):
        mine = pl.ds(pl.multiple_of(ex * TILE, TILE), TILE)

        def one(i, carry):
            to = lax.rem(ex + i, n_exp)
            theirs = pl.ds(pl.multiple_of(to * TILE, TILE), TILE)
            remote(send.at[c, theirs], recv.at[c, mine], all_s.at[c], all_r.at[c], {"expert": to}).start()
            return carry

        lax.fori_loop(1, n_exp, one, 0)
        pltpu.make_async_copy(send.at[c, mine], recv.at[c, mine], all_r.at[c]).start()

    def dispatch(c):
        shifts[c].wait_recv()
        x = inc[c]
        send[c, :, 0:WIDE] = (dot(pick_a[...], x) * gate_a).astype(BF16)
        stacked = jnp.concatenate([x[:, q * FOLD:(q + 1) * FOLD] for q in range(4)], axis=0)
        send[c, :, WIDE:WIDE + FOLD] = (dot(pick_b[...], stacked) * gate_b).astype(BF16)
        exchange(c, True)

    dispatch(0)

    target, source = iota((padded, rows), 0), iota((padded, rows), 1)
    sender = lax.shift_right_logical(target * 3277, 16)
    index = target - sender * cap
    same = sender == lax.shift_right_logical(source, 4)
    at = jnp.bitwise_and(source, TILE - 1)
    place_a[...] = ones_where(same & (index == at)).astype(BF16)
    tail = same & (index == TILE + jnp.bitwise_and(at, 3))
    for q in range(4):
        place_b[q] = ones_where(tail & (lax.shift_right_logical(at, 2) == q)).astype(BF16)

    for c in range(1, chunks):
        dispatch(c)

    load_hidden.wait()
    for i in range(units // FOLD):
        piece = hid[:, i * FOLD:(i + 1) * FOLD].astype(F32)
        piece = jnp.concatenate([piece, jnp.zeros((padded - slots, FOLD), F32)], axis=0)
        hid_t[i * FOLD:(i + 1) * FOLD, :] = piece.T.astype(BF16)

    halves_x = (pl.ds(0, half_x), pl.ds(half_x, half_x))
    halves_z = (pl.ds(0, half_z), pl.ds(half_z, block - half_z))

    def z_rows(z, half):
        start = pl.multiple_of(z * block, TILE)
        return pl.ds(start, half_z) if half == 0 else pl.ds(start + half_z, block - half_z)

    def x_copies(c):
        a, b = halves_x

        def way(k, far, near, to):
            return (
                remote(part.at[c, x_far, far], xr1.at[c, k], x_s.at[c, k, 0], x_r.at[c, k, 0], to),
                remote(part.at[c, near[0], near[1]], xr2.at[c, k, near[1]], x_s.at[c, k, 1], x_r.at[c, k, 1], to),
                remote(part.at[c, near[0], far], xr2.at[c, k, far], x_s.at[c, k, 2], x_r.at[c, k, 2], to),
            )

        return way(0, a, (x_up, b), to_x_up), way(1, b, (x_down, a), to_x_down)

    def z_copies(c):
        def way(k, near, to):
            far_half = k
            far_rows, rest = halves_z[far_half], halves_z[1 - far_half]
            land = pl.ds(0, half_z if far_half == 0 else block - half_z)
            return (
                remote(col.at[c, z_rows(z_far, far_half)], zr1.at[c, k, land], z_s.at[c, k, 0], z_r.at[c, k, 0], to),
                remote(col.at[c, z_rows(near, 1 - far_half)], zr2.at[c, k, rest], z_s.at[c, k, 1], z_r.at[c, k, 1], to),
                remote(col.at[c, z_rows(near, far_half)], zr2.at[c, k, far_rows], z_s.at[c, k, 2], z_r.at[c, k, 2], to),
            )

        return way(0, z_up, to_z_up), way(1, z_down, to_z_down)

    xs, zs = [x_copies(c) for c in range(chunks)], [z_copies(c) for c in range(chunks)]

    def partial(c):
        pltpu.make_async_copy(recv.at[c], recv.at[c], all_r.at[c]).wait()
        head, tails = dot(place_a[...], recv[c, :, 0:WIDE]), recv[c, :, WIDE:WIDE + FOLD]
        for q in range(4):
            here = slice(c * WIDE + q * FOLD, c * WIDE + (q + 1) * FOLD)
            scaled[:, here] = (head[:, q * FOLD:(q + 1) * FOLD] + dot(place_b[q], tails)).astype(BF16)

        def group(z, carry):
            take = pl.ds(pl.multiple_of(z * RING * own_rows, TILE), RING * own_rows)
            out = dot(hid_t[take, :], scaled[:, c * WIDE:(c + 1) * WIDE])
            land = pl.ds(pl.multiple_of(z * block, TILE), block)
            for x in range(RING):
                mine = out[x * own_rows:(x + 1) * own_rows]
                both = jnp.concatenate([mine[:, :WIDE // 2], mine[:, WIDE // 2:]], axis=0)
                part[c, x, land, :] = both.astype(BF16)
            return carry

        lax.fori_loop(0, RING, group, 0)
        for step in (0, 1):
            for way in (0, 1):
                xs[c][way][step].start()

    def add(ref, at, other):
        ref[at] = (ref[at].astype(F32) + other.astype(F32)).astype(BF16)

    def relay_x(c):
        for way, near in ((0, x_up), (1, x_down)):
            xs[c][way][0].wait_recv()
            add(part, (c, near, halves_x[way]), xr1[c, way])
            xs[c][way][2].start()

    def column(c):
        for way in (0, 1):
            xs[c][way][1].wait_recv()
            xs[c][way][2].wait_recv()
        for z in range(RING):
            here = pl.ds(z * block, block)
            total = part[c, xi, here].astype(F32) + xr2[c, 0, here].astype(F32) + xr2[c, 1, here].astype(F32)
            col[c, here] = total.astype(BF16)
        for step in (0, 1):
            for way in (0, 1):
                zs[c][way][step].start()

    def relay_z(c):
        for way, near in ((0, z_up), (1, z_down)):
            size = half_z if way == 0 else block - half_z
            zs[c][way][0].wait_recv()
            add(col, (c, z_rows(near, way)), zr1[c, way, 0:size])
            zs[c][way][2].start()

    def store_dw(c):
        here = pl.ds(c * WIDE, WIDE)
        return pltpu.make_async_copy(dwv.at[:, here], dw_ref.at[0, 0, :, here], dw_sem.at[c])

    def finish(c):
        for way in (0, 1):
            zs[c][way][1].wait_recv()
            zs[c][way][2].wait_recv()
        here = pl.ds(pl.multiple_of(zi * block, TILE), block)
        total = col[c, here].astype(F32) + zr2[c, 0].astype(F32) + zr2[c, 1].astype(F32)
        dwv[:, c * WIDE:c * WIDE + WIDE // 2] = total[:own_rows]
        dwv[:, c * WIDE + WIDE // 2:(c + 1) * WIDE] = total[own_rows:]
        store_dw(c).start()

    store_gh = pltpu.make_async_copy(ghv, gh_ref.at[0, 0, 0], gh_sem)
    edges = list(range(0, units, 2 * FOLD)) + [units]
    pieces = list(zip(edges[:-1], edges[1:]))

    def hidden_grad(part_of, of):
        for low, high in pieces[part_of::of]:
            out = lax.dot_general(
                scaled[0:slots, :], wv[low:high, :], (((1,), (1,)), ((), ())), preferred_element_type=F32
            )
            ghv[:, low:high] = out.astype(BF16)

    for c in range(chunks + 3):
        if c < chunks:
            partial(c)
            relay_x(c)
            if c == chunks - 1:
                load_w.wait()
        if c >= chunks:
            hidden_grad(c - chunks, 3)
        if c >= 1 and c - 1 < chunks:
            column(c - 1)
        if c >= 2 and c - 2 < chunks:
            relay_z(c - 2)
        if c >= 3 and c - 3 < chunks:
            finish(c - 3)
    store_gh.start()

    for c in range(chunks):
        shifts[c].wait_send()
        sent = send.at[c, pl.ds(0, rows - TILE)]
        pltpu.make_async_copy(sent, sent, all_s.at[c]).wait()
        for ways in (xs[c], zs[c]):
            for way in ways:
                for copy in way:
                    copy.wait_send()
        store_dw(c).wait()
    store_gh.wait()


def shards(counts, grad_out, routes, gates, hidden, w_down):
    n_sec, n_dp, n_exp = counts
    tok, width = grad_out.shape[1:]
    slots, units = hidden.shape[3:]
    own_rows = units // n_dp
    block = 2 * own_rows
    chunks = width // WIDE
    padded = -(-slots // FOLD) * FOLD
    rows = TILE * n_exp
    half_x = RING // 2 * block
    half_z = (block // TILE + 1) // 2 * TILE
    half = WIDE // 2
    anywhere, vmem = pl.BlockSpec(memory_space=pl.ANY), pl.BlockSpec(memory_space=pltpu.VMEM)
    dma = pltpu.SemaphoreType.DMA
    return pl.pallas_call(
        functools.partial(kernel, counts),
        out_shape=(
            jax.ShapeDtypeStruct((1, 1, 1, slots, units), BF16),
            jax.ShapeDtypeStruct((1, 1, own_rows, width), F32),
        ),
        in_specs=[anywhere, vmem, vmem, anywhere, anywhere],
        out_specs=(anywhere, anywhere),
        scratch_shapes=[
            pltpu.VMEM((chunks, tok, WIDE), BF16),
            pltpu.VMEM((chunks, rows, WIDE + FOLD), BF16),
            pltpu.VMEM((chunks, rows, WIDE + FOLD), BF16),
            pltpu.VMEM((rows, tok), BF16),
            pltpu.VMEM((rows, 4 * tok), BF16),
            pltpu.VMEM((padded, rows), BF16),
            pltpu.VMEM((4, padded, rows), BF16),
            pltpu.VMEM((padded, width), BF16),
            pltpu.VMEM((slots, units), BF16),
            pltpu.VMEM((units, padded), BF16),
            pltpu.VMEM((units, width), BF16),
            pltpu.VMEM((chunks, RING, RING * block, half), BF16),
            pltpu.VMEM((chunks, 2, half_x, half), BF16),
            pltpu.VMEM((chunks, 2, RING * block, half), BF16),
            pltpu.VMEM((chunks, RING * block, half), BF16),
            pltpu.VMEM((chunks, 2, half_z, half), BF16),
            pltpu.VMEM((chunks, 2, block, half), BF16),
            pltpu.VMEM((slots, units), BF16),
            pltpu.VMEM((own_rows, width), F32),
            dma((2,)),
            dma((chunks,)),
            dma((chunks,)),
            dma((chunks,)),
            dma((chunks,)),
            dma((chunks, 2, 3)),
            dma((chunks, 2, 3)),
            dma((chunks, 2, 3)),
            dma((chunks, 2, 3)),
            dma((chunks,)),
            dma,
        ],
        compiler_params=pltpu.CompilerParams(
            collective_id=0, has_side_effects=True, vmem_limit_bytes=48 * 1024 * 1024
        ),
        name="relayed_backward",
    )(grad_out, routes, gates, hidden, w_down)


def solution(mesh):
    counts = tuple(mesh.shape[axis] for axis in ("section", "dp", "expert"))
    placed = (
        P("section", ("dp", "expert"), None),
        P("section", ("dp", "expert"), None),
        P("section", ("dp", "expert"), None),
        P("section", "dp", "expert", None, None),
        P("section", "expert", None, None),
    )
    return jax.shard_map(
        functools.partial(shards, counts),
        mesh=mesh,
        in_specs=placed,
        out_specs=(P("section", "dp", "expert", None, None), P("section", "expert", "dp", None)),
        check_vma=False,
    )
```

time: 259 us -> 113 us (0.44)
  waiting for transfers between devices: 143 us -> 0 us
  Pallas kernels: 0 us -> 106 us
  blocking collectives: 52.9 us -> 0 us
  local copies, waits for them, and re-layouts: 23.9 us -> 5.56 us
  between operations: 14.1 us -> 0.65 us
  matrix products: 12.4 us -> 0 us
  starting transfers between devices: 6.81 us -> 0 us
  other arithmetic: 4.93 us -> 0 us
    unnamed x2 -> x0, waiting for transfers between devices: 141 us -> none
    pallas_call x0 -> x1, Pallas kernels: none -> 106 us  [shards(): pl.pallas_call(functools.partial(kernel, counts), out_shape=(jax.ShapeDty...]
    all_to_all x1 -> x0, blocking collectives: 52.9 us -> none  [shards(): lax.all_to_all(outgoing, 'expert', split_axis=0, concat_axis=0, tiled=True)]
    dot_general x2 -> x0, matrix products: 12.4 us -> none  [the longest x1 7.15 us: shards(): lax.dot_general(saved, scaled, (((0,), (0,)), ((), ())), preferred_elemen...]
    ppermute x1 -> x0, starting transfers between devices: 6.77 us -> none  [shifted(): return lax.ppermute(value, axis, pairs)]
    unnamed x7 -> x8, local copies, waits for them, and re-layouts: 12.3 us -> 5.56 us
    mul x5 -> x0, local copies, waits for them, and re-layouts: 5.63 us -> none  [the longest x3 5.38 us: dispatch_block(): weights[:, :, None] * rows[:, None, :].astype(jnp.float32)]
    reshape x3 -> x0, local copies, waits for them, and re-layouts: 5.51 us -> none  [the longest x1 3.21 us: dispatch_block(): return buffer.reshape(count, width, rows.shape[1])]
  transfers between devices with their start and end apart: 2 -> 0, of which waited for: 2 -> 0; matrix products, arithmetic and copies ran while one was open for 4% -> 0% of each run, Pallas kernels for 0% -> 0%
where the time goes in v1:
time: 113 us
  Pallas kernels  106 us (94%)
  local copies, waits for them, and re-layouts  5.56 us (5%)
    pallas_call x1, Pallas kernels, shards(): pl.pallas_call(functools.partial(kernel, counts), out_shape=(jax.ShapeDty...  106 us
    unnamed x8, local copies, waits for them, and re-layouts  5.56 us

profile of v1, /device:TPU:1, one launch (start us, length us, event | category | flops | bytes accessed | tf_op | source)
XLA Modules:
  0.0 112.5 jit_solution(11262037747905659031)
XLA Ops:
  0.6 0.8 copy.7.routes_ref
  1.4 0.8 copy.8.gates_ref
  2.2 0.0 copy-start
  2.2 1.2 %copy-done = bf16[1,1,1,320,1408]{4,3,2,1,0:T(8,128)(2,1)S(1)} copy-done((bf16[1,1,1,320,1408]{4,3,2,1,0:T(8,128)(2,1)S(1)}, bf16[1,1,1,320,1408]{4,3,2,1,0:T(8,128)(2,1)}, u32[]{:S(2)}) %copy-start) | copy-done | bytes 901144
  3.4 0.0 copy-start.1
  3.4 1.0 copy-done.1
  4.4 106.3 %relayed_backward.1 = (bf16[1,1,1,320,1408]{4,3,2,1,0:T(8,128)(2,1)S(1)}, f32[1,1,88,2048]{3,2,1,0:T(8,128)S(1)}) custom-call(bf16[1,128,2048]{2,1,0:T(8,128)(2,1)S(1)} %copy-done.1, s32[1,128,2]{2,1,0:T(8,128)S(1)} %copy.7.routes_ref, f32[1,128,2]{2,1,0:T(8,128)S(1)} %copy.8.gates_ref, bf16[1,1,1,320,1408]{4,3,2,1,0:T(8,128)(2,1)S(1)} %copy-done, ...), custom_call_target="tpu_custom_call" | custom-call | tf_op jit(solution)/shard_map/relayed_backward/pallas_call | solution.py:300
  110.8 0.9 copy.11
  111.7 0.9 copy.12
Async XLA Ops:
  2.2 1.2 %copy-start = (bf16[1,1,1,320,1408]{4,3,2,1,0:T(8,128)(2,1)S(1)}, bf16[1,1,1,320,1408]{4,3,2,1,0:T(8,128)(2,1)}, u32[]{:S(2)}) copy-start(bf16[1,1,1,320,1408]{4,3,2,1,0:T(8,128)(2,1)} %hidden_ref.1) | copy-start | bytes 2703364
  3.4 1.0 copy-start.1

commit v2 on v1

v2 whole, which is shorter than its diff:
```python
import functools

import jax
import jax.numpy as jnp
from jax import lax
from jax.experimental import pallas as pl
from jax.experimental.pallas import tpu as pltpu
from jax.sharding import PartitionSpec as P

MESH = pl.DeviceIdType.MESH
RING = 4
WIDE = 512
FOLD = 128
TILE = 16
VMEM_BYTES = 60 * 1024 * 1024
BF16, F32 = jnp.bfloat16, jnp.float32


def iota(shape, dim):
    return lax.broadcasted_iota(jnp.int32, shape, dim)


def ones_where(mask):
    return jnp.where(mask, 1.0, 0.0)


def dot(left, right):
    return jnp.dot(left, right, preferred_element_type=F32)


def kernel(
    counts, grad_ref, routes_ref, gates_ref, hidden_ref, w_ref, gh_ref, dw_ref,
    inc, send, recv, pick_a, pick_b, place_a, place_b, scaled, hid, turned, far_hid, left, right, wv,
    out_x, in_x, own, col, zr1, zr2, ghv, dwv,
    in_sem, shift_s, shift_r, all_s, all_r, hid_s, hid_r, row_s, row_r, x_s, x_r, z_s, z_r, dw_sem, gh_sem,
):
    n_sec, n_dp, n_exp = counts
    tok, width = grad_ref.shape[1:]
    slots, units = hid.shape
    cap = slots // n_exp
    own_rows = units // n_dp
    group = RING * own_rows
    chunks = width // WIDE
    half = WIDE // 2
    padded = turned.shape[1]
    rows = TILE * n_exp

    sec, dp, ex = lax.axis_index("section"), lax.axis_index("dp"), lax.axis_index("expert")
    xi, zi = lax.rem(dp, RING), lax.div(dp, RING)
    odd = lax.rem(xi, 2)
    beside = (xi + 1 - 2 * odd, lax.rem(xi + RING - 1 + 2 * odd, RING))
    x_far, z_far = lax.rem(xi + 2, RING), lax.rem(zi + 2, RING)
    z_up, z_down = lax.rem(zi + 1, RING), lax.rem(zi + RING - 1, RING)
    to_x = tuple({"dp": zi * RING + x} for x in beside)
    to_z = tuple({"dp": z * RING + xi} for z in (z_up, z_down))
    before, after = {"section": lax.rem(sec + n_sec - 1, n_sec)}, {"section": lax.rem(sec + 1, n_sec)}

    barrier = pltpu.get_barrier_semaphore()

    def greet(to):
        pl.semaphore_signal(barrier, inc=1, device_id=to, device_id_type=MESH)

    for to in (before, after, *to_x, *to_z):
        greet(to)

    def greet_expert(i, carry):
        greet({"expert": lax.rem(ex + i, n_exp)})
        return carry

    lax.fori_loop(1, n_exp, greet_expert, 0)
    load_hidden = pltpu.make_async_copy(hidden_ref.at[0, 0, 0], hid, in_sem.at[0])
    load_w = pltpu.make_async_copy(w_ref.at[0, 0], wv, in_sem.at[1])
    load_hidden.start()
    pl.semaphore_wait(barrier, 6 + n_exp - 1)

    def remote(source, target, send_sem, recv_sem, to):
        return pltpu.make_async_remote_copy(
            src_ref=source, dst_ref=target, send_sem=send_sem, recv_sem=recv_sem, device_id=to, device_id_type=MESH
        )

    shifts = [
        remote(grad_ref.at[0, :, pl.ds(c * WIDE, WIDE)], inc.at[c], shift_s.at[c], shift_r.at[c], before)
        for c in range(chunks)
    ]
    for copy in shifts:
        copy.start()

    named, gates = routes_ref[0].astype(F32), gates_ref[0]
    expert = lax.shift_right_logical(iota((rows, tok), 0), 4).astype(F32)
    place = jnp.bitwise_and(iota((rows, tok), 0), TILE - 1)
    first, second = named[0:1] == expert, named[1:2] == expert
    active = ones_where(first | second)
    gate = jnp.where(first, gates[0:1], jnp.where(second, gates[1:2], 0.0))
    earlier = ones_where(iota((tok, tok), 0) < iota((tok, tok), 1)).astype(BF16)
    slot = dot(active.astype(BF16), earlier)
    hit_a = jnp.where(slot == place.astype(F32), active, 0.0)
    hit_b = jnp.where(slot == (TILE + jnp.bitwise_and(place, 3)).astype(F32), active, 0.0)
    gate_a = jnp.sum(hit_a * gate, axis=1, keepdims=True)
    gate_b = jnp.sum(hit_b * gate, axis=1, keepdims=True)
    pick_a[...] = hit_a.astype(BF16)
    quarter = lax.shift_right_logical(place, 2)
    for q in range(4):
        pick_b[:, q * tok:(q + 1) * tok] = jnp.where(quarter == q, hit_b, 0.0).astype(BF16)

    def exchange(c):
        mine = pl.ds(pl.multiple_of(ex * TILE, TILE), TILE)

        def one(i, carry):
            to = lax.rem(ex + i, n_exp)
            theirs = pl.ds(pl.multiple_of(to * TILE, TILE), TILE)
            remote(send.at[c, theirs], recv.at[c, mine], all_s.at[c], all_r.at[c], {"expert": to}).start()
            return carry

        lax.fori_loop(1, n_exp, one, 0)
        pltpu.make_async_copy(send.at[c, mine], recv.at[c, mine], all_r.at[c]).start()

    def dispatch(c):
        shifts[c].wait_recv()
        x = inc[c]
        send[c, :, 0:WIDE] = (dot(pick_a[...], x) * gate_a).astype(BF16)
        stacked = jnp.concatenate([x[:, q * FOLD:(q + 1) * FOLD] for q in range(4)], axis=0)
        send[c, :, WIDE:WIDE + FOLD] = (dot(pick_b[...], stacked) * gate_b).astype(BF16)
        exchange(c)

    top, low = pl.ds(0, group), pl.ds(group, group)
    mine_k, other_k = pl.ds(0, padded), pl.ds(padded, padded)
    give_hidden = [
        (
            remote(far_hid, left.at[h, top, other_k], hid_s.at[h, 0], hid_r.at[h, 0], to_x[h]),
            remote(left.at[1 - h, top, mine_k], left.at[h, low, other_k], hid_s.at[h, 1], hid_r.at[h, 1], to_x[h]),
        )
        for h in (0, 1)
    ]

    def turn_hidden():
        load_hidden.wait()
        for i in range(units // FOLD):
            piece = hid[:, i * FOLD:(i + 1) * FOLD].astype(F32)
            piece = jnp.concatenate([piece, jnp.zeros((padded - slots, FOLD), F32)], axis=0)
            turned[i * FOLD:(i + 1) * FOLD, :] = piece.T

        def of_owner(x):
            starts = [pl.multiple_of((z * RING + x) * own_rows, 8) for z in range(RING)]
            return jnp.concatenate([turned[pl.ds(start, own_rows), :] for start in starts], axis=0).astype(BF16)

        far_hid[...] = of_owner(x_far)
        for h in (0, 1):
            give_hidden[h][0].start()
        for h in (0, 1):
            left[1 - h, 0:group, 0:padded] = of_owner(beside[h])
            give_hidden[h][1].start()
        mine = of_owner(xi)
        for h in (0, 1):
            left[h, group:2 * group, 0:padded] = mine

    give_rows = [
        [
            remote(right.at[c, h, pl.ds(0, slots)], right.at[c, h, pl.ds(padded, slots)],
                   row_s.at[c, h], row_r.at[c, h], to_x[h])
            for h in (0, 1)
        ]
        for c in range(chunks)
    ]
    give_sums = [
        [remote(out_x.at[c, h], in_x.at[c, h], x_s.at[c, h], x_r.at[c, h], to_x[1 - h]) for h in (0, 1)]
        for c in range(chunks)
    ]

    def z_copies(c):
        return [
            (
                remote(col.at[c, k, z_far], zr1.at[c, k], z_s.at[c, k, 0], z_r.at[c, k, 0], to_z[k]),
                remote(col.at[c, 1 - k, near], zr2.at[c, k, 1 - k], z_s.at[c, k, 1], z_r.at[c, k, 1], to_z[k]),
                remote(col.at[c, k, near], zr2.at[c, k, k], z_s.at[c, k, 2], z_r.at[c, k, 2], to_z[k]),
            )
            for k, near in ((0, z_up), (1, z_down))
        ]

    zs = [z_copies(c) for c in range(chunks)]

    def collect(c):
        pltpu.make_async_copy(recv.at[c], recv.at[c], all_r.at[c]).wait()
        head, tails = dot(place_a[...], recv[c, :, 0:WIDE]), recv[c, :, WIDE:WIDE + FOLD]
        for q in range(4):
            block = (head[:, q * FOLD:(q + 1) * FOLD] + dot(place_b[q], tails)).astype(BF16)
            h, at = q // 2, q % 2 * FOLD
            right[c, h, 0:padded, at:at + FOLD] = block
            scaled[:, c * WIDE + q * FOLD:c * WIDE + (q + 1) * FOLD] = block[0:slots]
        for h in (0, 1):
            give_rows[c][h].start()

    def multiply(c):
        for h in (0, 1):
            if c == 0:
                for copy in give_hidden[h]:
                    copy.wait_recv()
            give_rows[c][h].wait_recv()
            for which in (0, 1):
                out = dot(left[h, which * group:(which + 1) * group, :], right[c, h])
                for z in range(RING):
                    mine = out[z * own_rows:(z + 1) * own_rows]
                    both = jnp.concatenate([mine[:, :FOLD], mine[:, FOLD:]], axis=0)
                    if which == 0:
                        out_x[c, h, z] = both.astype(BF16)
                    else:
                        own[c, h, z] = both
                if which == 0:
                    give_sums[c][h].start()

    def column(c):
        for h in (0, 1):
            give_sums[c][h].wait_recv()
            col[c, h] = (own[c, h] + in_x[c, h].astype(F32)).astype(BF16)
        for step in (0, 1):
            for way in (0, 1):
                zs[c][way][step].start()

    def relay(c):
        for way, near in ((0, z_up), (1, z_down)):
            zs[c][way][0].wait_recv()
            col[c, way, near] = (col[c, way, near].astype(F32) + zr1[c, way].astype(F32)).astype(BF16)
            zs[c][way][2].start()

    def store_dw(c):
        here = pl.ds(c * WIDE, WIDE)
        return pltpu.make_async_copy(dwv.at[:, here], dw_ref.at[0, 0, :, here], dw_sem.at[c])

    def finish(c):
        for way in (0, 1):
            zs[c][way][1].wait_recv()
            zs[c][way][2].wait_recv()
        for h in (0, 1):
            total = col[c, h, zi].astype(F32) + zr2[c, 0, h].astype(F32) + zr2[c, 1, h].astype(F32)
            at = c * WIDE + h * half
            dwv[:, at:at + FOLD] = total[:own_rows]
            dwv[:, at + FOLD:at + half] = total[own_rows:]
        store_dw(c).start()

    store_gh = pltpu.make_async_copy(ghv, gh_ref.at[0, 0, 0], gh_sem)
    edges = list(range(0, units, half)) + [units]
    pieces = list(zip(edges[:-1], edges[1:]))

    def hidden_grad(part_of):
        for low_edge, high_edge in pieces[part_of::3]:
            out = lax.dot_general(
                scaled[...], wv[low_edge:high_edge, :], (((1,), (1,)), ((), ())), preferred_element_type=F32
            )
            ghv[:, low_edge:high_edge] = out.astype(BF16)

    dispatch(0)
    turn_hidden()
    load_w.start()

    target, source = iota((padded, rows), 0), iota((padded, rows), 1)
    sender = lax.shift_right_logical(target * 3277, 16)
    index = target - sender * cap
    same = sender == lax.shift_right_logical(source, 4)
    at = jnp.bitwise_and(source, TILE - 1)
    place_a[...] = ones_where(same & (index == at)).astype(BF16)
    tail = same & (index == TILE + jnp.bitwise_and(at, 3))
    for q in range(4):
        place_b[q] = ones_where(tail & (lax.shift_right_logical(at, 2) == q)).astype(BF16)
    for c in range(chunks):
        for h in (0, 1):
            right[c, h, padded + slots:2 * padded, :] = jnp.zeros((padded - slots, half), BF16)

    dispatch(1)
    for c in range(chunks):
        collect(c)
        if c == 0:
            for later in range(2, chunks):
                dispatch(later)
        if c >= 1:
            column(c - 1)
        if c == chunks - 1:
            load_w.wait()
            hidden_grad(0)
        multiply(c)
        if c >= 1:
            relay(c - 1)
        if c >= 2:
            finish(c - 2)
    hidden_grad(1)
    column(chunks - 1)
    hidden_grad(2)
    store_gh.start()
    finish(chunks - 2)
    relay(chunks - 1)
    finish(chunks - 1)

    for h in (0, 1):
        for copy in give_hidden[h]:
            copy.wait_send()
    for c in range(chunks):
        shifts[c].wait_send()
        sent = send.at[c, pl.ds(0, rows - TILE)]
        pltpu.make_async_copy(sent, sent, all_s.at[c]).wait()
        for copy in (*give_rows[c], *give_sums[c], *zs[c][0], *zs[c][1]):
            copy.wait_send()
        store_dw(c).wait()
    store_gh.wait()


def shards(counts, grad_out, routes, gates, hidden, w_down):
    n_sec, n_dp, n_exp = counts
    tok, width = grad_out.shape[1:]
    slots, units = hidden.shape[3:]
    own_rows = units // n_dp
    block = 2 * own_rows
    group = RING * own_rows
    chunks = width // WIDE
    padded = -(-slots // FOLD) * FOLD
    rows = TILE * n_exp
    half = WIDE // 2
    anywhere, vmem = pl.BlockSpec(memory_space=pl.ANY), pl.BlockSpec(memory_space=pltpu.VMEM)
    dma = pltpu.SemaphoreType.DMA
    return pl.pallas_call(
        functools.partial(kernel, counts),
        out_shape=(
            jax.ShapeDtypeStruct((1, 1, 1, slots, units), BF16),
            jax.ShapeDtypeStruct((1, 1, own_rows, width), F32),
        ),
        in_specs=[anywhere, vmem, vmem, anywhere, anywhere],
        out_specs=(anywhere, anywhere),
        scratch_shapes=[
            pltpu.VMEM((chunks, tok, WIDE), BF16),
            pltpu.VMEM((chunks, rows, WIDE + FOLD), BF16),
            pltpu.VMEM((chunks, rows, WIDE + FOLD), BF16),
            pltpu.VMEM((rows, tok), BF16),
            pltpu.VMEM((rows, 4 * tok), BF16),
            pltpu.VMEM((padded, rows), BF16),
            pltpu.VMEM((4, padded, rows), BF16),
            pltpu.VMEM((slots, width), BF16),
            pltpu.VMEM((slots, units), BF16),
            pltpu.VMEM((units, padded), F32),
            pltpu.VMEM((group, padded), BF16),
            pltpu.VMEM((2, 2 * group, 2 * padded), BF16),
            pltpu.VMEM((chunks, 2, 2 * padded, half), BF16),
            pltpu.VMEM((units, width), BF16),
            pltpu.VMEM((chunks, 2, RING, block, FOLD), BF16),
            pltpu.VMEM((chunks, 2, RING, block, FOLD), BF16),
            pltpu.VMEM((chunks, 2, RING, block, FOLD), F32),
            pltpu.VMEM((chunks, 2, RING, block, FOLD), BF16),
            pltpu.VMEM((chunks, 2, block, FOLD), BF16),
            pltpu.VMEM((chunks, 2, 2, block, FOLD), BF16),
            pltpu.VMEM((slots, units), BF16),
            pltpu.VMEM((own_rows, width), F32),
            dma((2,)),
            dma((chunks,)),
            dma((chunks,)),
            dma((chunks,)),
            dma((chunks,)),
            dma((2, 2)),
            dma((2, 2)),
            dma((chunks, 2)),
            dma((chunks, 2)),
            dma((chunks, 2)),
            dma((chunks, 2)),
            dma((chunks, 2, 3)),
            dma((chunks, 2, 3)),
            dma((chunks,)),
            dma,
        ],
        compiler_params=pltpu.CompilerParams(
            collective_id=0, has_side_effects=True, vmem_limit_bytes=VMEM_BYTES
        ),
        name="relayed_backward",
    )(grad_out, routes.transpose(0, 2, 1), gates.transpose(0, 2, 1), hidden, w_down)


def solution(mesh):
    counts = tuple(mesh.shape[axis] for axis in ("section", "dp", "expert"))
    placed = (
        P("section", ("dp", "expert"), None),
        P("section", ("dp", "expert"), None),
        P("section", ("dp", "expert"), None),
        P("section", "dp", "expert", None, None),
        P("section", "expert", None, None),
    )
    return jax.shard_map(
        functools.partial(shards, counts),
        mesh=mesh,
        in_specs=placed,
        out_specs=(P("section", "dp", "expert", None, None), P("section", "expert", "dp", None)),
        check_vma=False,
    )
```

time: 113 us -> 98.5 us (0.87)
  the two profiles are of different devices: /device:TPU:1 before, /device:TPU:64 now
where the time goes in v2:
time: 98.5 us; the launch traced here: 98.3 us
  Pallas kernels  93.4 us (95%)
  local copies, waits for them, and re-layouts  4.18 us (4%)
    pallas_call x1, Pallas kernels, shards(): pl.pallas_call(functools.partial(kernel, counts), out_shape=(jax.ShapeDty...  93.4 us
    unnamed x2, local copies, waits for them, and re-layouts  4.18 us

profile of v2, /device:TPU:64, one launch (start us, length us, event | category | flops | bytes accessed | tf_op | source)
XLA Modules:
  0.0 98.3 jit_solution(285742539561970671)
XLA Ops:
  0.6 93.4 %relayed_backward.1 = (bf16[1,1,1,320,1408]{4,3,2,1,0:T(8,128)(2,1)}, f32[1,1,88,2048]{3,2,1,0:T(8,128)}) custom-call(bf16[1,128,2048]{2,1,0:T(8,128)(2,1)} %grad_ref.1, s32[1,2,128]{2,1,0:T(2,128)} %bitcast.2, f32[1,2,128]{2,1,0:T(2,128)} %bitcast.3, bf16[1,1,1,320,1408]{4,3,2,1,0:T(8,128)(2,1)} %hidden_ref.1, bf16[1,1,1408,2048]{3,2,1,0:T(8,128)(2,1)} %w_ref.1), custom_call_target="tpu_custom_call" | custom-call | tf_op jit(solution)/shard_map/relayed_backward/pallas_call | solution.py:317
  94.1 2.2 %copy.9 = bf16[1,1,1,320,1408]{4,3,2,1,0:T(8,128)(2,1)} copy(bf16[1,1,1,320,1408]{4,3,2,1,0:T(8,128)(2,1)} %get-tuple-element.4) | data formatting | bytes 1802240
  96.2 2.0 %copy.10 = f32[1,1,88,2048]{3,2,1,0:T(8,128)} copy(f32[1,1,88,2048]{3,2,1,0:T(8,128)} %get-tuple-element.5) | data formatting | bytes 1441792

commit v3 on v2

v3 whole, which is shorter than its diff:
```python
import functools

import jax
import jax.numpy as jnp
from jax import lax
from jax.experimental import pallas as pl
from jax.experimental.pallas import tpu as pltpu
from jax.sharding import PartitionSpec as P

MESH = pl.DeviceIdType.MESH
RING = 4
WIDE = 512
NARROW = 256
FOLD = 128
TILE = 16
LEAD = 2
FOLDINGS = ((4, 2), (2, 3))
KINDS = {WIDE: 0, NARROW: 1}
VMEM_BYTES = 48 * 1024 * 1024
BF16, F32 = jnp.bfloat16, jnp.float32


def iota(shape, dim):
    return lax.broadcasted_iota(jnp.int32, shape, dim)


def ones_where(mask):
    return jnp.where(mask, 1.0, 0.0)


def dot(left, right):
    return jnp.dot(left, right, preferred_element_type=F32)


def cut_up(width):
    wide = (width - 2 * NARROW) // WIDE
    widths = [NARROW] + [WIDE] * wide + [NARROW]
    return widths, [sum(widths[:c]) for c in range(len(widths))]


def block_rows(wide, own_rows):
    return 2 * own_rows if wide == WIDE else -(-own_rows // TILE) * TILE


def kernel(
    counts, grad_ref, routes_ref, gates_ref, hidden_ref, w_ref, gh_ref, dw_ref,
    inc, send, recv, pick_a, pick_bs, place_a, place_bs, scaled, hid, turned, far_hid, left, right, wv,
    out_x, in_x, own, col, zr1, zr2, ghv, dwv,
    in_sem, shift_s, shift_r, all_s, all_r, hid_s, hid_r, row_s, row_r, x_s, x_r, z_s, z_r, dw_sem, gh_sem,
):
    n_sec, n_dp, n_exp = counts
    tok, width = grad_ref.shape[1:]
    slots, units = hid.shape
    cap = slots // n_exp
    own_rows = units // n_dp
    group = RING * own_rows
    widths, starts_at = cut_up(width)
    chunks = len(widths)
    padded = turned.shape[1]
    rows = TILE * n_exp

    sec, dp, ex = lax.axis_index("section"), lax.axis_index("dp"), lax.axis_index("expert")
    xi, zi = lax.rem(dp, RING), lax.div(dp, RING)
    odd = lax.rem(xi, 2)
    beside = (xi + 1 - 2 * odd, lax.rem(xi + RING - 1 + 2 * odd, RING))
    x_far, z_far = lax.rem(xi + 2, RING), lax.rem(zi + 2, RING)
    z_up, z_down = lax.rem(zi + 1, RING), lax.rem(zi + RING - 1, RING)
    to_x = tuple({"dp": zi * RING + x} for x in beside)
    to_z = tuple({"dp": z * RING + xi} for z in (z_up, z_down))
    before, after = {"section": lax.rem(sec + n_sec - 1, n_sec)}, {"section": lax.rem(sec + 1, n_sec)}

    barrier = pltpu.get_barrier_semaphore()

    def greet(to):
        pl.semaphore_signal(barrier, inc=1, device_id=to, device_id_type=MESH)

    for to in (before, after, *to_x, *to_z):
        greet(to)

    def greet_expert(i, carry):
        greet({"expert": lax.rem(ex + i, n_exp)})
        return carry

    lax.fori_loop(1, n_exp, greet_expert, 0)
    load_hidden = pltpu.make_async_copy(hidden_ref.at[0, 0, 0], hid, in_sem.at[0])
    load_w = pltpu.make_async_copy(w_ref.at[0, 0], wv, in_sem.at[1])
    load_hidden.start()
    def remote(source, target, send_sem, recv_sem, to):
        return pltpu.make_async_remote_copy(
            src_ref=source, dst_ref=target, send_sem=send_sem, recv_sem=recv_sem, device_id=to, device_id_type=MESH
        )

    def columns(c):
        return pl.ds(starts_at[c], widths[c])

    def cells(c):
        return pl.ds(0, widths[c] + FOLD)

    shifts = [
        remote(grad_ref.at[0, :, columns(c)], inc.at[:, columns(c)], shift_s.at[c], shift_r.at[c], before)
        for c in range(chunks)
    ]
    named, gates = routes_ref[0].astype(F32), gates_ref[0]
    expert = lax.shift_right_logical(iota((rows, tok), 0), 4).astype(F32)
    place = jnp.bitwise_and(iota((rows, tok), 0), TILE - 1)
    first, second = named[0:1] == expert, named[1:2] == expert
    active = ones_where(first | second)
    gate = jnp.where(first, gates[0:1], jnp.where(second, gates[1:2], 0.0))
    earlier = ones_where(iota((tok, tok), 0) < iota((tok, tok), 1)).astype(BF16)
    slot = dot(active.astype(BF16), earlier)
    hit_a = jnp.where(slot == place.astype(F32), active, 0.0)
    gate_a = jnp.sum(hit_a * gate, axis=1, keepdims=True)
    pick_a[...] = hit_a.astype(BF16)
    gate_bs = []
    for pick_b, (folds, depth_bits) in zip(pick_bs, FOLDINGS):
        late = TILE + jnp.bitwise_and(place, TILE // folds - 1)
        hit_b = jnp.where(slot == late.astype(F32), active, 0.0)
        gate_bs.append(jnp.sum(hit_b * gate, axis=1, keepdims=True))
        fold = lax.shift_right_logical(place, depth_bits)
        for q in range(folds):
            pick_b[:, q * tok:(q + 1) * tok] = jnp.where(fold == q, hit_b, 0.0).astype(BF16)

    def rows_of(e):
        return pl.ds(pl.multiple_of(e * TILE, TILE), TILE)

    def exchange(c):
        def one(i, carry):
            to = lax.rem(ex + lax.rem(i, 2) * ((i + 1) // 2) + (1 - lax.rem(i, 2)) * (n_exp - i // 2), n_exp)

            remote(
                send.at[c, rows_of(to), cells(c)], recv.at[c, rows_of(ex), cells(c)],
                all_s.at[c], all_r.at[c], {"expert": to},
            ).start()
            return carry

        lax.fori_loop(1, n_exp, one, 0)
        pltpu.make_async_copy(
            send.at[c, rows_of(ex), cells(c)], recv.at[c, rows_of(ex), cells(c)], all_r.at[c]
        ).start()

    def dispatch(c):
        shifts[c].wait_recv()
        if c + 1 < chunks:
            shifts[c + 1].start()
        wide, kind = widths[c], KINDS[widths[c]]
        x = inc[:, columns(c)]
        send[c, :, 0:wide] = (dot(pick_a[...], x) * gate_a).astype(BF16)
        stacked = jnp.concatenate([x[:, q * FOLD:(q + 1) * FOLD] for q in range(wide // FOLD)], axis=0)
        send[c, :, wide:wide + FOLD] = (dot(pick_bs[kind][...], stacked) * gate_bs[kind]).astype(BF16)

    top, low = pl.ds(0, group), pl.ds(group, group)
    mine_k, other_k = pl.ds(0, padded), pl.ds(padded, padded)
    give_hidden = [
        (
            remote(far_hid, left.at[h, top, other_k], hid_s.at[h, 0], hid_r.at[h, 0], to_x[h]),
            remote(left.at[1 - h, top, mine_k], left.at[h, low, other_k], hid_s.at[h, 1], hid_r.at[h, 1], to_x[h]),
        )
        for h in (0, 1)
    ]

    def turn_hidden():
        load_hidden.wait()
        for i in range(units // FOLD):
            piece = hid[:, i * FOLD:(i + 1) * FOLD].astype(F32)
            piece = jnp.concatenate([piece, jnp.zeros((padded - slots, FOLD), F32)], axis=0)
            turned[i * FOLD:(i + 1) * FOLD, :] = piece.T

        def of_owner(x):
            starts = [pl.multiple_of((z * RING + x) * own_rows, 8) for z in range(RING)]
            return jnp.concatenate([turned[pl.ds(start, own_rows), :] for start in starts], axis=0).astype(BF16)

        far_hid[...] = of_owner(x_far)
        for h in (0, 1):
            give_hidden[h][0].start()
        for h in (0, 1):
            left[1 - h, 0:group, 0:padded] = of_owner(beside[h])
            give_hidden[h][1].start()
        mine = of_owner(xi)
        for h in (0, 1):
            left[h, group:2 * group, 0:padded] = mine

    give_rows = [
        [
            remote(right[c].at[h, pl.ds(0, slots)], right[c].at[h, pl.ds(padded, slots)],
                   row_s.at[c, h], row_r.at[c, h], to_x[h])
            for h in (0, 1)
        ]
        for c in range(chunks)
    ]
    give_sums = [
        [remote(out_x[c].at[h], in_x[c].at[h], x_s.at[c, h], x_r.at[c, h], to_x[1 - h]) for h in (0, 1)]
        for c in range(chunks)
    ]

    def z_copies(c):
        return [
            (
                remote(col[c].at[k, z_far], zr1[c].at[k], z_s.at[c, k, 0], z_r.at[c, k, 0], to_z[k]),
                remote(col[c].at[1 - k, near], zr2[c].at[k, 1 - k], z_s.at[c, k, 1], z_r.at[c, k, 1], to_z[k]),
                remote(col[c].at[k, near], zr2[c].at[k, k], z_s.at[c, k, 2], z_r.at[c, k, 2], to_z[k]),
            )
            for k, near in ((0, z_up), (1, z_down))
        ]

    zs = [z_copies(c) for c in range(chunks)]

    def collect(c):
        arrived = recv.at[c, :, cells(c)]
        pltpu.make_async_copy(arrived, arrived, all_r.at[c]).wait()
        wide, start, place_b = widths[c], starts_at[c], place_bs[KINDS[widths[c]]]
        head, tails = dot(place_a[...], recv[c, :, 0:wide]), recv[c, :, wide:wide + FOLD]
        folds = wide // FOLD
        for q in range(folds):
            block = (head[:, q * FOLD:(q + 1) * FOLD] + dot(place_b[q], tails)).astype(BF16)
            h, at = q // (folds // 2), q % (folds // 2) * FOLD
            right[c][h, 0:padded, at:at + FOLD] = block
            scaled[:, start + q * FOLD:start + (q + 1) * FOLD] = block[0:slots]
        for h in (0, 1):
            give_rows[c][h].start()

    def multiply(c):
        for h in (0, 1):
            if c == 0:
                for copy in give_hidden[h]:
                    copy.wait_recv()
            give_rows[c][h].wait_recv()
            for which in (0, 1):
                out = dot(left[h, which * group:(which + 1) * group, :], right[c][h])
                for z in range(RING):
                    mine = out[z * own_rows:(z + 1) * own_rows]
                    if widths[c] == WIDE:
                        mine = jnp.concatenate([mine[:, :FOLD], mine[:, FOLD:]], axis=0)
                    fill = block_rows(widths[c], own_rows) - mine.shape[0]
                    if fill:
                        mine = jnp.concatenate([mine, jnp.zeros((fill, FOLD), F32)], axis=0)
                    if which == 0:
                        out_x[c][h, z] = mine.astype(BF16)
                    else:
                        own[c][h, z] = mine
                if which == 0:
                    give_sums[c][h].start()

    def column(c):
        for h in (0, 1):
            give_sums[c][h].wait_recv()
            col[c][h] = (own[c][h] + in_x[c][h].astype(F32)).astype(BF16)
        for step in (0, 1):
            for way in (0, 1):
                zs[c][way][step].start()

    def relay(c):
        for way, near in ((0, z_up), (1, z_down)):
            zs[c][way][0].wait_recv()
            col[c][way, near] = (col[c][way, near].astype(F32) + zr1[c][way].astype(F32)).astype(BF16)
            zs[c][way][2].start()

    def store_dw(c):
        here = columns(c)
        return pltpu.make_async_copy(dwv.at[:, here], dw_ref.at[0, 0, :, here], dw_sem.at[c])

    def finish(c):
        for way in (0, 1):
            zs[c][way][1].wait_recv()
            zs[c][way][2].wait_recv()
        for h in (0, 1):
            total = col[c][h, zi].astype(F32) + zr2[c][0, h].astype(F32) + zr2[c][1, h].astype(F32)
            at = starts_at[c] + h * (widths[c] // 2)
            dwv[:, at:at + FOLD] = total[:own_rows]
            if widths[c] == WIDE:
                dwv[:, at + FOLD:at + 2 * FOLD] = total[own_rows:]
        store_dw(c).start()

    store_gh = pltpu.make_async_copy(ghv, gh_ref.at[0, 0, 0], gh_sem)
    edges = list(range(0, units, 2 * FOLD)) + [units]
    pieces = list(zip(edges[:-1], edges[1:]))

    def hidden_grad(part_of):
        for low_edge, high_edge in pieces[part_of::3]:
            out = lax.dot_general(
                scaled[...], wv[low_edge:high_edge, :], (((1,), (1,)), ((), ())), preferred_element_type=F32
            )
            ghv[:, low_edge:high_edge] = out.astype(BF16)

    pl.semaphore_wait(barrier, 6 + n_exp - 1)
    shifts[0].start()
    turn_hidden()
    dispatch(0)
    exchange(0)
    load_w.start()

    target, source = iota((padded, rows), 0), iota((padded, rows), 1)
    sender = lax.shift_right_logical(target * 3277, 16)
    index = target - sender * cap
    same = sender == lax.shift_right_logical(source, 4)
    at = jnp.bitwise_and(source, TILE - 1)
    place_a[...] = ones_where(same & (index == at)).astype(BF16)
    for place_b, (folds, depth_bits) in zip(place_bs, FOLDINGS):
        late = same & (index == TILE + jnp.bitwise_and(at, TILE // folds - 1))
        for q in range(folds):
            place_b[q] = ones_where(late & (lax.shift_right_logical(at, depth_bits) == q)).astype(BF16)
    for c in range(chunks):
        for h in (0, 1):
            right[c][h, padded + slots:2 * padded, :] = jnp.zeros((padded - slots, widths[c] // 2), BF16)

    for c in range(1, LEAD):
        dispatch(c)
        exchange(c)
    for c in range(chunks):
        collect(c)
        if c + LEAD < chunks:
            dispatch(c + LEAD)
            exchange(c + LEAD)
        if c >= 2:
            relay(c - 2)
        if c == chunks - 1:
            load_w.wait()
            hidden_grad(0)
        if c >= 1:
            column(c - 1)
        multiply(c)
        if c >= 3:
            finish(c - 3)
    relay(chunks - 2)
    hidden_grad(1)
    column(chunks - 1)
    hidden_grad(2)
    store_gh.start()
    finish(chunks - 3)
    relay(chunks - 1)
    finish(chunks - 2)
    finish(chunks - 1)

    for h in (0, 1):
        for copy in give_hidden[h]:
            copy.wait_send()
    for c in range(chunks):
        shifts[c].wait_send()
        sent = send.at[c, pl.ds(0, rows - TILE), cells(c)]
        pltpu.make_async_copy(sent, sent, all_s.at[c]).wait()
        for copy in (*give_rows[c], *give_sums[c], *zs[c][0], *zs[c][1]):
            copy.wait_send()
        store_dw(c).wait()
    store_gh.wait()


def shards(counts, grad_out, routes, gates, hidden, w_down):
    n_sec, n_dp, n_exp = counts
    tok, width = grad_out.shape[1:]
    slots, units = hidden.shape[3:]
    own_rows = units // n_dp
    group = RING * own_rows
    widths, _ = cut_up(width)
    chunks = len(widths)
    padded = -(-slots // FOLD) * FOLD
    rows = TILE * n_exp
    blocks = [block_rows(wide, own_rows) for wide in widths]
    hbm, anywhere = pl.BlockSpec(memory_space=pltpu.HBM), pl.BlockSpec(memory_space=pl.ANY)
    vmem = pl.BlockSpec(memory_space=pltpu.VMEM)
    dma = pltpu.SemaphoreType.DMA
    return pl.pallas_call(
        functools.partial(kernel, counts),
        out_shape=(
            jax.ShapeDtypeStruct((1, 1, 1, slots, units), BF16),
            jax.ShapeDtypeStruct((1, 1, own_rows, width), F32),
        ),
        in_specs=[hbm, vmem, vmem, hbm, hbm],
        out_specs=(anywhere, anywhere),
        scratch_shapes=[
            pltpu.VMEM((tok, width), BF16),
            pltpu.VMEM((chunks, rows, WIDE + FOLD), BF16),
            pltpu.VMEM((chunks, rows, WIDE + FOLD), BF16),
            pltpu.VMEM((rows, tok), BF16),
            tuple(pltpu.VMEM((rows, folds * tok), BF16) for folds, _ in FOLDINGS),
            pltpu.VMEM((padded, rows), BF16),
            tuple(pltpu.VMEM((folds, padded, rows), BF16) for folds, _ in FOLDINGS),
            pltpu.VMEM((slots, width), BF16),
            pltpu.VMEM((slots, units), BF16),
            pltpu.VMEM((units, padded), F32),
            pltpu.VMEM((group, padded), BF16),
            pltpu.VMEM((2, 2 * group, 2 * padded), BF16),
            tuple(pltpu.VMEM((2, 2 * padded, wide // 2), BF16) for wide in widths),
            pltpu.VMEM((units, width), BF16),
            tuple(pltpu.VMEM((2, RING, block, FOLD), BF16) for block in blocks),
            tuple(pltpu.VMEM((2, RING, block, FOLD), BF16) for block in blocks),
            tuple(pltpu.VMEM((2, RING, block, FOLD), F32) for block in blocks),
            tuple(pltpu.VMEM((2, RING, block, FOLD), BF16) for block in blocks),
            tuple(pltpu.VMEM((2, block, FOLD), BF16) for block in blocks),
            tuple(pltpu.VMEM((2, 2, block, FOLD), BF16) for block in blocks),
            pltpu.VMEM((slots, units), BF16),
            pltpu.VMEM((own_rows, width), F32),
            dma((2,)),
            dma((chunks,)),
            dma((chunks,)),
            dma((chunks,)),
            dma((chunks,)),
            dma((2, 2)),
            dma((2, 2)),
            dma((chunks, 2)),
            dma((chunks, 2)),
            dma((chunks, 2)),
            dma((chunks, 2)),
            dma((chunks, 2, 3)),
            dma((chunks, 2, 3)),
            dma((chunks,)),
            dma,
        ],
        compiler_params=pltpu.CompilerParams(
            collective_id=0, has_side_effects=True, vmem_limit_bytes=VMEM_BYTES
        ),
        name="relayed_backward",
    )(grad_out, routes.transpose(0, 2, 1), gates.transpose(0, 2, 1), hidden, w_down)


def solution(mesh):
    counts = tuple(mesh.shape[axis] for axis in ("section", "dp", "expert"))
    placed = (
        P("section", ("dp", "expert"), None),
        P("section", ("dp", "expert"), None),
        P("section", ("dp", "expert"), None),
        P("section", "dp", "expert", None, None),
        P("section", "expert", None, None),
    )
    return jax.shard_map(
        functools.partial(shards, counts),
        mesh=mesh,
        in_specs=placed,
        out_specs=(P("section", "dp", "expert", None, None), P("section", "expert", "dp", None)),
        check_vma=False,
    )
```

time: 98.5 us -> 93.4 us (0.948)
  the two profiles are of different devices: /device:TPU:64 before, /device:TPU:2 now
where the time goes in v3:
time: 93.4 us; the launch traced here: 93.1 us
  Pallas kernels  87.1 us (93%)
  local copies, waits for them, and re-layouts  5.34 us (6%)
    pallas_call x1, Pallas kernels, shards(): pl.pallas_call(functools.partial(kernel, counts), out_shape=(jax.ShapeDty...  87.1 us
    unnamed x10, local copies, waits for them, and re-layouts  5.34 us

profile of v3, /device:TPU:2, one launch (start us, length us, event | category | flops | bytes accessed | tf_op | source)
XLA Modules:
  0.0 93.1 jit_solution(4084334106144812097)
XLA Ops:
  0.6 0.0 copy-start
  0.6 1.2 %copy-done = bf16[1,1,1,320,1408]{4,3,2,1,0:T(8,128)(2,1)S(1)} copy-done((bf16[1,1,1,320,1408]{4,3,2,1,0:T(8,128)(2,1)S(1)}, bf16[1,1,1,320,1408]{4,3,2,1,0:T(8,128)(2,1)}, u32[]{:S(2)}) %copy-start) | copy-done | bytes 901144
  1.8 0.0 copy-start.1
  1.8 1.0 %copy-done.1 = bf16[1,128,2048]{2,1,0:T(8,128)(2,1)S(1)} copy-done((bf16[1,128,2048]{2,1,0:T(8,128)(2,1)S(1)}, bf16[1,128,2048]{2,1,0:T(8,128)(2,1)}, u32[]{:S(2)}) %copy-start.1) | copy-done | bytes 524312
  2.8 0.0 copy-start.2
  2.8 0.7 copy-done.2
  3.5 0.0 copy-start.3
  3.5 0.7 copy-done.3
  4.2 87.1 %relayed_backward.1 = (bf16[1,1,1,320,1408]{4,3,2,1,0:T(8,128)(2,1)S(1)}, f32[1,1,88,2048]{3,2,1,0:T(8,128)S(1)}) custom-call(bf16[1,128,2048]{2,1,0:T(8,128)(2,1)S(1)} %copy-done.1, s32[1,2,128]{2,1,0:T(2,128)S(1)} %bitcast.2, f32[1,2,128]{2,1,0:T(2,128)S(1)} %bitcast.3, bf16[1,1,1,320,1408]{4,3,2,1,0:T(8,128)(2,1)S(1)} %copy-done, ...), custom_call_target="tpu_custom_call" | custom-call | tf_op jit(solution)/shard_map/relayed_backward/pallas_call | solution.py:360
  91.4 0.9 copy.9
  92.3 0.9 copy.10
Async XLA Ops:
  0.6 1.2 %copy-start = (bf16[1,1,1,320,1408]{4,3,2,1,0:T(8,128)(2,1)S(1)}, bf16[1,1,1,320,1408]{4,3,2,1,0:T(8,128)(2,1)}, u32[]{:S(2)}) copy-start(bf16[1,1,1,320,1408]{4,3,2,1,0:T(8,128)(2,1)} %hidden_ref.1) | copy-start | bytes 2703364
  1.8 1.0 %copy-start.1 = (bf16[1,128,2048]{2,1,0:T(8,128)(2,1)S(1)}, bf16[1,128,2048]{2,1,0:T(8,128)(2,1)}, u32[]{:S(2)}) copy-start(bf16[1,128,2048]{2,1,0:T(8,128)(2,1)} %grad_ref.1) | copy-start | bytes 1572868
  2.8 0.7 copy-start.2
  3.5 0.7 copy-start.3

commit v4 on v3

--- a/solution.py
+++ b/solution.py
@@ -215,8 +215,8 @@
             h, at = q // (folds // 2), q % (folds // 2) * FOLD
             right[c][h, 0:padded, at:at + FOLD] = block
             scaled[:, start + q * FOLD:start + (q + 1) * FOLD] = block[0:slots]
-        for h in (0, 1):
-            give_rows[c][h].start()
+            if q % (folds // 2) == folds // 2 - 1:
+                give_rows[c][h].start()
 
     def multiply(c):
         for h in (0, 1):
@@ -244,9 +244,8 @@
         for h in (0, 1):
             give_sums[c][h].wait_recv()
             col[c][h] = (own[c][h] + in_x[c][h].astype(F32)).astype(BF16)
-        for step in (0, 1):
-            for way in (0, 1):
-                zs[c][way][step].start()
+            zs[c][h][0].start()
+            zs[c][1 - h][1].start()
 
     def relay(c):
         for way, near in ((0, z_up), (1, z_down)):

time: 93.4 us -> 99.2 us (1.062)
  the two profiles are of different devices: /device:TPU:2 before, /device:TPU:1 now
where the time goes in v4:
time: 99.2 us; the launch traced here: 98.2 us
  Pallas kernels  92.2 us (93%)
  local copies, waits for them, and re-layouts  5.34 us (5%)
    pallas_call x1, Pallas kernels, shards(): pl.pallas_call(functools.partial(kernel, counts), out_shape=(jax.ShapeDty...  92.2 us
    unnamed x10, local copies, waits for them, and re-layouts  5.34 us

profile of v4, /device:TPU:1, one launch (start us, length us, event | category | flops | bytes accessed | tf_op | source)
XLA Modules:
  0.0 98.2 jit_solution(3403024876383694338)
XLA Ops:
  0.6 0.0 copy-start
  0.6 1.2 %copy-done = bf16[1,1,1,320,1408]{4,3,2,1,0:T(8,128)(2,1)S(1)} copy-done((bf16[1,1,1,320,1408]{4,3,2,1,0:T(8,128)(2,1)S(1)}, bf16[1,1,1,320,1408]{4,3,2,1,0:T(8,128)(2,1)}, u32[]{:S(2)}) %copy-start) | copy-done | bytes 901144
  1.8 0.0 copy-start.1
  1.8 1.0 %copy-done.1 = bf16[1,128,2048]{2,1,0:T(8,128)(2,1)S(1)} copy-done((bf16[1,128,2048]{2,1,0:T(8,128)(2,1)S(1)}, bf16[1,128,2048]{2,1,0:T(8,128)(2,1)}, u32[]{:S(2)}) %copy-start.1) | copy-done | bytes 524312
  2.8 0.0 copy-start.2
  2.8 0.7 copy-done.2
  3.5 0.0 copy-start.3
  3.5 0.7 copy-done.3
  4.2 92.2 %relayed_backward.1 = (bf16[1,1,1,320,1408]{4,3,2,1,0:T(8,128)(2,1)S(1)}, f32[1,1,88,2048]{3,2,1,0:T(8,128)S(1)}) custom-call(bf16[1,128,2048]{2,1,0:T(8,128)(2,1)S(1)} %copy-done.1, s32[1,2,128]{2,1,0:T(2,128)S(1)} %bitcast.2, f32[1,2,128]{2,1,0:T(2,128)S(1)} %bitcast.3, bf16[1,1,1,320,1408]{4,3,2,1,0:T(8,128)(2,1)S(1)} %copy-done, ...), custom_call_target="tpu_custom_call" | custom-call | tf_op jit(solution)/shard_map/relayed_backward/pallas_call | solution.py:359
  96.4 0.9 copy.9
  97.3 0.9 copy.10
Async XLA Ops:
  0.6 1.2 %copy-start = (bf16[1,1,1,320,1408]{4,3,2,1,0:T(8,128)(2,1)S(1)}, bf16[1,1,1,320,1408]{4,3,2,1,0:T(8,128)(2,1)}, u32[]{:S(2)}) copy-start(bf16[1,1,1,320,1408]{4,3,2,1,0:T(8,128)(2,1)} %hidden_ref.1) | copy-start | bytes 2703364
  1.8 1.0 %copy-start.1 = (bf16[1,128,2048]{2,1,0:T(8,128)(2,1)S(1)}, bf16[1,128,2048]{2,1,0:T(8,128)(2,1)}, u32[]{:S(2)}) copy-start(bf16[1,128,2048]{2,1,0:T(8,128)(2,1)} %grad_ref.1) | copy-start | bytes 1572868
  2.8 0.7 copy-start.2
  3.5 0.7 copy-start.3
